TPU v7x, 128 devices: a whole 4x4x4 slice. The times are simulated.
128 devices in a mesh: scen: 4 (over y), row: 4 (over x), col: 8 (over z, core).
Axes of the slice: x: 4, y: 4, z: 4, core: 2. Of those that a mesh axis runs over, the one named last changes fastest.
Arguments:
- tech_matrix: bfloat16 [8, 8192, 4096], P('scen', 'row', 'col'), may hold values from -0.02734375 to 0.02734375
- recourse_matrix: bfloat16 [8, 8192, 12288], P('scen', 'row', 'col'), may hold values from -0.02734375 to 0.02734375
- first_cost: float32 [4096], P('col'), may hold values from -60 to 60
- recourse_cost: float32 [8, 12288], P('scen', 'col'), may hold values from -60 to 60
- demand: float32 [8, 8192], P('scen', 'row'), may hold values from -60 to 60
- first_upper: float32 [4096], P('col'), may hold values from 0.5 to 4
- recourse_upper: float32 [8, 12288], P('scen', 'col'), may hold values from 0.5 to 4
- first_start: float32 [4096], P('col'), may hold values from 0 to 1
- recourse_start: float32 [8, 12288], P('scen', 'col'), may hold values from 0 to 1
- dual_start: float32 [8, 8192], P('scen', 'row'), may hold values from 0 to 1
Outputs:
- first_section: float32 [4096], P('col')
- recourse: float32 [8, 12288], P('scen', 'col')
- duals: float32 [8, 8192], P('scen', 'row')
- primal_weight: float32 [], replicated
All inputs are finite; a program needn't handle non-finite values.
Results may differ from a plain program's by a relative error of at most 0.0003.
Values sent between devices are 32-bit elements; how exact they have to be, the bound alone decides.
A program may use at most 64 MiB of HBM per device.

v0:
```python
import jax
import jax.numpy as jnp
from jax import lax
from jax.sharding import PartitionSpec as P

ITERS = 4


STEP_SCALE = 0.8
EPSILON = 1e-06


def split_pair(vector):
    upper_part = lax.optimization_barrier(vector.astype(jnp.bfloat16))
    lower_part = (vector - upper_part.astype(jnp.float32)).astype(jnp.bfloat16)
    return jnp.stack([upper_part, lower_part], 1)


def forward(matrix, vector):
    stacked = split_pair(vector)
    return jnp.einsum("src,skc->skr", matrix, stacked, preferred_element_type=jnp.float32).sum(1)


def backward(matrix, vector):
    stacked = split_pair(vector)
    return jnp.einsum("src,skr->skc", matrix, stacked, preferred_element_type=jnp.float32).sum(1)


def reweight(weight_now, primal_move, dual_move):
    return jnp.exp(
        0.25 * jnp.log((dual_move + EPSILON) / (primal_move + EPSILON)) + 0.5 * jnp.log(weight_now)
    )


def local(
    tech_matrix,
    recourse_matrix,
    first_cost,
    recourse_cost,
    demand,
    first_upper,
    recourse_upper,
    first_start,
    recourse_start,
    dual_start,
):
    first_lead = jnp.logical_and(lax.axis_index("scen") == 0, lax.axis_index("row") == 0)
    recourse_lead = lax.axis_index("row") == 0
    dual_lead = lax.axis_index("col") == 0

    def iterate(counter, carry):
        first_now, recourse_now, duals_now, weight_now, pending = carry
        first_part = backward(tech_matrix, duals_now).sum(0)
        recourse_part = backward(recourse_matrix, duals_now)
        first_grad = lax.psum(first_part, ("scen", "row"))
        recourse_grad = lax.psum(recourse_part, "row")
        step_primal = STEP_SCALE / weight_now
        step_dual = STEP_SCALE * weight_now
        first_new = jnp.clip(first_now - step_primal * (first_cost - first_grad), 0.0, first_upper)
        recourse_new = jnp.clip(
            recourse_now - step_primal * (recourse_cost - recourse_grad), 0.0, recourse_upper
        )
        first_bar = 2.0 * first_new - first_now
        recourse_bar = 2.0 * recourse_new - recourse_now
        first_wide = jnp.broadcast_to(first_bar, (duals_now.shape[0], first_bar.shape[0]))
        activity_part = forward(tech_matrix, first_wide) + forward(recourse_matrix, recourse_bar)
        primal_move = jnp.where(first_lead, jnp.sum((first_new - first_now) ** 2), 0.0)
        primal_move = primal_move + jnp.where(
            recourse_lead, jnp.sum((recourse_new - recourse_now) ** 2), 0.0
        )
        activity = lax.psum(activity_part, "col")
        duals_new = jnp.maximum(0.0, duals_now + step_dual * (demand - activity))
        dual_full = jnp.sum((duals_new - duals_now) ** 2)
        dual_move = jnp.where(dual_lead, dual_full, 0.0)
        primal_total, dual_total = lax.psum((primal_move, dual_move), ("scen", "row", "col"))
        weight_new = reweight(weight_now, primal_total, dual_total)
        return (first_new, recourse_new, duals_new, weight_new, pending)

    start = (
        first_start,
        recourse_start,
        dual_start,
        jnp.ones((), jnp.float32),
        jnp.zeros((2,), jnp.float32),
    )
    first_now, recourse_now, duals_now, weight_now, pending = lax.fori_loop(
        0, ITERS, iterate, start
    )
    return (first_now, recourse_now, duals_now, weight_now)


def solution(mesh):
    in_specs = (
        P("scen", "row", "col"),
        P("scen", "row", "col"),
        P("col"),
        P("scen", "col"),
        P("scen", "row"),
        P("col"),
        P("scen", "col"),
        P("col"),
        P("scen", "col"),
        P("scen", "row"),
    )
    out_specs = (P("col"), P("scen", "col"), P("scen", "row"), P())
    return jax.shard_map(local, mesh=mesh, in_specs=in_specs, out_specs=out_specs, check_vma=False)
```

profile of v0, /device:TPU:0, one launch (start us, length us, event | category | flops | bytes accessed | tf_op | source)
XLA Modules:
  0.0 663.5 jit_solution(2243110865199056280)
XLA Ops:
  2.7 659.0 %while.16 = (s32[]{:T(128)}, f32[512]{0:T(512)S(1)}, f32[2,1536]{1,0:T(2,128)S(1)}, f32[2,2048]{1,0:T(2,128)S(1)}, f32[]{:T(128)}, /*index=5*/bf16[2,2048,512]{2...) while((s32[]{:T(128)}, f32[512]{0:T(512)S(1)}, ...), condition=%wide.region_13.14_spmd, body=%wide.region_0.13_spmd.sunk | while | flops 67333632 | bytes 34314776 | solution.py:86
  2.9 2.9 fusion.37
  5.8 6.3 convolution_reduce_fusion.6
  12.1 16.9 %psum.39 = f32[2,1536]{1,0:T(2,128)S(1)} all-reduce(f32[2,1536]{1,0:T(2,128)S(1)} %convolution_reduce_fusion.6), channel_id=1, replica_groups=mesh['scen'=4,'row'=4,'col'=8] {'row'}, use_global_device_ids=true, to_apply=%region_4.0 | all-reduce | flops 3072 | bytes 24576 | tf_op jit(solution)/shard_map/while/body/eval_jaxpr/psum | solution.py:56
  29.1 37.6 %psum.38 = f32[512]{0:T(512)S(1)} all-reduce(f32[512]{0:T(512)S(1)} %fusion.37), channel_id=1, replica_groups=mesh['scen'=4,'row'=4,'col'=8] {'scen','row'}, use_global_device_ids=true, to_apply=%region_2.0 | all-reduce | flops 512 | bytes 4096 | tf_op jit(solution)/shard_map/while/body/eval_jaxpr/psum | solution.py:55
  69.4 3.4 convolution_reduce_fusion.7
  72.8 7.9 %convolution_reduce_fusion.8 = f32[2,2048]{1,0:T(2,128)S(1)} fusion(bf16[2,2048,1536]{2,1,0:T(8,128)(2,1)} %get-tuple-element.289, bf16[2,1,1536]{2,1,0:T(2,128)(2,1)S(1)} %copy.36, bf16[2,1,1536]{2,1,0:T(2,128)(2,1)S(1)} %copy.37), kind=kOutput, calls=%fused_computation.clone.1 | convolution fusion | flops 25194496 | bytes 12611584 | tf_op jit(solution)/shard_map/while/body/eval_jaxpr/src,skc->skr/dot_general | solution.py:21
  80.8 24.7 %psum.40 = f32[2,2048]{1,0:T(2,128)S(1)} all-reduce(f32[2,2048]{1,0:T(2,128)S(1)} %add.42), channel_id=1, replica_groups=mesh['scen'=4,'row'=4,'col'=8] {'col'}, use_global_device_ids=true, to_apply=%region_7.7 | all-reduce | flops 4096 | bytes 32768 | tf_op jit(solution)/shard_map/while/body/eval_jaxpr/psum | solution.py:71
  106.8 62.5 %all-reduce.2 = (f32[]{:T(128)}, f32[]{:T(128)}) all-reduce(f32[]{:T(128)S(6)} %select_n.13, f32[]{:T(128)S(6)} %add.43), channel_id=1, replica_groups=mesh['scen'=4,'row'=4,'col'=8] {'scen','row','col'}, use_global_device_ids=true, to_apply=%region_9.9 | all-reduce | flops 2 | bytes 16 | tf_op jit(solution)/shard_map/while/body/eval_jaxpr/psum | solution.py:75
  173.7 6.3 convolution_reduce_fusion.6
  180.1 14.3 %psum.39 = f32[2,1536]{1,0:T(2,128)S(1)} all-reduce(f32[2,1536]{1,0:T(2,128)S(1)} %convolution_reduce_fusion.6), channel_id=1, replica_groups=mesh['scen'=4,'row'=4,'col'=8] {'row'}, use_global_device_ids=true, to_apply=%region_4.0 | all-reduce | flops 3072 | bytes 24576 | tf_op jit(solution)/shard_map/while/body/eval_jaxpr/psum | solution.py:56
  194.4 37.2 %psum.38 = f32[512]{0:T(512)S(1)} all-reduce(f32[512]{0:T(512)S(1)} %fusion.37), channel_id=1, replica_groups=mesh['scen'=4,'row'=4,'col'=8] {'scen','row'}, use_global_device_ids=true, to_apply=%region_2.0 | all-reduce | flops 512 | bytes 4096 | tf_op jit(solution)/shard_map/while/body/eval_jaxpr/psum | solution.py:55
  234.3 3.4 convolution_reduce_fusion.7
  237.7 7.9 %convolution_reduce_fusion.8 = f32[2,2048]{1,0:T(2,128)S(1)} fusion(bf16[2,2048,1536]{2,1,0:T(8,128)(2,1)} %get-tuple-element.289, bf16[2,1,1536]{2,1,0:T(2,128)(2,1)S(1)} %copy.36, bf16[2,1,1536]{2,1,0:T(2,128)(2,1)S(1)} %copy.37), kind=kOutput, calls=%fused_computation.clone.1 | convolution fusion | flops 25194496 | bytes 12611584 | tf_op jit(solution)/shard_map/while/body/eval_jaxpr/src,skc->skr/dot_general | solution.py:21
  245.7 23.6 %psum.40 = f32[2,2048]{1,0:T(2,128)S(1)} all-reduce(f32[2,2048]{1,0:T(2,128)S(1)} %add.42), channel_id=1, replica_groups=mesh['scen'=4,'row'=4,'col'=8] {'col'}, use_global_device_ids=true, to_apply=%region_7.7 | all-reduce | flops 4096 | bytes 32768 | tf_op jit(solution)/shard_map/while/body/eval_jaxpr/psum | solution.py:71
  270.5 62.5 %all-reduce.2 = (f32[]{:T(128)}, f32[]{:T(128)}) all-reduce(f32[]{:T(128)S(6)} %select_n.13, f32[]{:T(128)S(6)} %add.43), channel_id=1, replica_groups=mesh['scen'=4,'row'=4,'col'=8] {'scen','row','col'}, use_global_device_ids=true, to_apply=%region_9.9 | all-reduce | flops 2 | bytes 16 | tf_op jit(solution)/shard_map/while/body/eval_jaxpr/psum | solution.py:75
  334.6 2.9 fusion.37
  337.4 6.3 convolution_reduce_fusion.6
  343.8 14.3 %psum.39 = f32[2,1536]{1,0:T(2,128)S(1)} all-reduce(f32[2,1536]{1,0:T(2,128)S(1)} %convolution_reduce_fusion.6), channel_id=1, replica_groups=mesh['scen'=4,'row'=4,'col'=8] {'row'}, use_global_device_ids=true, to_apply=%region_4.0 | all-reduce | flops 3072 | bytes 24576 | tf_op jit(solution)/shard_map/while/body/eval_jaxpr/psum | solution.py:56
  358.1 37.2 %psum.38 = f32[512]{0:T(512)S(1)} all-reduce(f32[512]{0:T(512)S(1)} %fusion.37), channel_id=1, replica_groups=mesh['scen'=4,'row'=4,'col'=8] {'scen','row'}, use_global_device_ids=true, to_apply=%region_2.0 | all-reduce | flops 512 | bytes 4096 | tf_op jit(solution)/shard_map/while/body/eval_jaxpr/psum | solution.py:55
  398.0 3.4 convolution_reduce_fusion.7
  401.4 7.9 %convolution_reduce_fusion.8 = f32[2,2048]{1,0:T(2,128)S(1)} fusion(bf16[2,2048,1536]{2,1,0:T(8,128)(2,1)} %get-tuple-element.289, bf16[2,1,1536]{2,1,0:T(2,128)(2,1)S(1)} %copy.36, bf16[2,1,1536]{2,1,0:T(2,128)(2,1)S(1)} %copy.37), kind=kOutput, calls=%fused_computation.clone.1 | convolution fusion | flops 25194496 | bytes 12611584 | tf_op jit(solution)/shard_map/while/body/eval_jaxpr/src,skc->skr/dot_general | solution.py:21
  409.4 23.6 %psum.40 = f32[2,2048]{1,0:T(2,128)S(1)} all-reduce(f32[2,2048]{1,0:T(2,128)S(1)} %add.42), channel_id=1, replica_groups=mesh['scen'=4,'row'=4,'col'=8] {'col'}, use_global_device_ids=true, to_apply=%region_7.7 | all-reduce | flops 4096 | bytes 32768 | tf_op jit(solution)/shard_map/while/body/eval_jaxpr/psum | solution.py:71
  434.2 62.5 %all-reduce.2 = (f32[]{:T(128)}, f32[]{:T(128)}) all-reduce(f32[]{:T(128)S(6)} %select_n.13, f32[]{:T(128)S(6)} %add.43), channel_id=1, replica_groups=mesh['scen'=4,'row'=4,'col'=8] {'scen','row','col'}, use_global_device_ids=true, to_apply=%region_9.9 | all-reduce | flops 2 | bytes 16 | tf_op jit(solution)/shard_map/while/body/eval_jaxpr/psum | solution.py:75
  498.2 2.9 fusion.37
  501.1 6.3 convolution_reduce_fusion.6
  507.5 14.3 %psum.39 = f32[2,1536]{1,0:T(2,128)S(1)} all-reduce(f32[2,1536]{1,0:T(2,128)S(1)} %convolution_reduce_fusion.6), channel_id=1, replica_groups=mesh['scen'=4,'row'=4,'col'=8] {'row'}, use_global_device_ids=true, to_apply=%region_4.0 | all-reduce | flops 3072 | bytes 24576 | tf_op jit(solution)/shard_map/while/body/eval_jaxpr/psum | solution.py:56
  521.7 37.2 %psum.38 = f32[512]{0:T(512)S(1)} all-reduce(f32[512]{0:T(512)S(1)} %fusion.37), channel_id=1, replica_groups=mesh['scen'=4,'row'=4,'col'=8] {'scen','row'}, use_global_device_ids=true, to_apply=%region_2.0 | all-reduce | flops 512 | bytes 4096 | tf_op jit(solution)/shard_map/while/body/eval_jaxpr/psum | solution.py:55
  561.7 3.4 convolution_reduce_fusion.7
  565.1 7.9 %convolution_reduce_fusion.8 = f32[2,2048]{1,0:T(2,128)S(1)} fusion(bf16[2,2048,1536]{2,1,0:T(8,128)(2,1)} %get-tuple-element.289, bf16[2,1,1536]{2,1,0:T(2,128)(2,1)S(1)} %copy.36, bf16[2,1,1536]{2,1,0:T(2,128)(2,1)S(1)} %copy.37), kind=kOutput, calls=%fused_computation.clone.1 | convolution fusion | flops 25194496 | bytes 12611584 | tf_op jit(solution)/shard_map/while/body/eval_jaxpr/src,skc->skr/dot_general | solution.py:21
  573.1 23.6 %psum.40 = f32[2,2048]{1,0:T(2,128)S(1)} all-reduce(f32[2,2048]{1,0:T(2,128)S(1)} %add.42), channel_id=1, replica_groups=mesh['scen'=4,'row'=4,'col'=8] {'col'}, use_global_device_ids=true, to_apply=%region_7.7 | all-reduce | flops 4096 | bytes 32768 | tf_op jit(solution)/shard_map/while/body/eval_jaxpr/psum | solution.py:71
  597.9 62.5 %all-reduce.2 = (f32[]{:T(128)}, f32[]{:T(128)}) all-reduce(f32[]{:T(128)S(6)} %select_n.13, f32[]{:T(128)S(6)} %add.43), channel_id=1, replica_groups=mesh['scen'=4,'row'=4,'col'=8] {'scen','row','col'}, use_global_device_ids=true, to_apply=%region_9.9 | all-reduce | flops 2 | bytes 16 | tf_op jit(solution)/shard_map/while/body/eval_jaxpr/psum | solution.py:75
  (126 shorter events, 13.7 us)
Async XLA Ops:
  2.7 64.0 %copy-start.6 = (f32[512]{0:T(512)S(1)}, f32[512]{0:T(512)}, u32[]{:S(2)}) copy-start(f32[512]{0:T(512)} %get-tuple-element.287) | copy-start | bytes 6148 | tf_op jit(solution)/shard_map/while
  2.7 64.0 %copy-start.7 = (f32[512]{0:T(512)S(1)}, f32[512]{0:T(512)}, u32[]{:S(2)}) copy-start(f32[512]{0:T(512)} %get-tuple-element.288) | copy-start | bytes 6148 | tf_op jit(solution)/shard_map/while
  2.7 65.2 %copy-start.3 = (f32[2,1536]{1,0:T(2,128)S(1)}, f32[2,1536]{1,0:T(2,128)}, u32[]{:S(2)}) copy-start(f32[2,1536]{1,0:T(2,128)} %get-tuple-element.290) | copy-start | bytes 36868 | tf_op jit(solution)/shard_map/while
  2.7 65.2 %copy-start.4 = (f32[2,1536]{1,0:T(2,128)S(1)}, f32[2,1536]{1,0:T(2,128)}, u32[]{:S(2)}) copy-start(f32[2,1536]{1,0:T(2,128)} %get-tuple-element.291) | copy-start | bytes 36868 | tf_op jit(solution)/shard_map/while
  12.1 93.4 %copy-start.2 = (f32[2,2048]{1,0:T(2,128)S(1)}, f32[2,2048]{1,0:T(2,128)}, u32[]{:S(2)}) copy-start(f32[2,2048]{1,0:T(2,128)} %get-tuple-element.292) | copy-start | bytes 49156 | tf_op jit(solution)/shard_map/while
  170.7 60.9 %copy-start.6 = (f32[512]{0:T(512)S(1)}, f32[512]{0:T(512)}, u32[]{:S(2)}) copy-start(f32[512]{0:T(512)} %get-tuple-element.287) | copy-start | bytes 6148 | tf_op jit(solution)/shard_map/while
  170.7 60.9 %copy-start.7 = (f32[512]{0:T(512)S(1)}, f32[512]{0:T(512)}, u32[]{:S(2)}) copy-start(f32[512]{0:T(512)} %get-tuple-element.288) | copy-start | bytes 6148 | tf_op jit(solution)/shard_map/while
  170.7 62.2 %copy-start.3 = (f32[2,1536]{1,0:T(2,128)S(1)}, f32[2,1536]{1,0:T(2,128)}, u32[]{:S(2)}) copy-start(f32[2,1536]{1,0:T(2,128)} %get-tuple-element.290) | copy-start | bytes 36868 | tf_op jit(solution)/shard_map/while
  170.7 62.2 %copy-start.4 = (f32[2,1536]{1,0:T(2,128)S(1)}, f32[2,1536]{1,0:T(2,128)}, u32[]{:S(2)}) copy-start(f32[2,1536]{1,0:T(2,128)} %get-tuple-element.291) | copy-start | bytes 36868 | tf_op jit(solution)/shard_map/while
  180.1 89.2 %copy-start.2 = (f32[2,2048]{1,0:T(2,128)S(1)}, f32[2,2048]{1,0:T(2,128)}, u32[]{:S(2)}) copy-start(f32[2,2048]{1,0:T(2,128)} %get-tuple-element.292) | copy-start | bytes 49156 | tf_op jit(solution)/shard_map/while
  334.4 60.9 %copy-start.6 = (f32[512]{0:T(512)S(1)}, f32[512]{0:T(512)}, u32[]{:S(2)}) copy-start(f32[512]{0:T(512)} %get-tuple-element.287) | copy-start | bytes 6148 | tf_op jit(solution)/shard_map/while
  334.4 60.9 %copy-start.7 = (f32[512]{0:T(512)S(1)}, f32[512]{0:T(512)}, u32[]{:S(2)}) copy-start(f32[512]{0:T(512)} %get-tuple-element.288) | copy-start | bytes 6148 | tf_op jit(solution)/shard_map/while
  334.4 62.2 %copy-start.3 = (f32[2,1536]{1,0:T(2,128)S(1)}, f32[2,1536]{1,0:T(2,128)}, u32[]{:S(2)}) copy-start(f32[2,1536]{1,0:T(2,128)} %get-tuple-element.290) | copy-start | bytes 36868 | tf_op jit(solution)/shard_map/while
  334.4 62.2 %copy-start.4 = (f32[2,1536]{1,0:T(2,128)S(1)}, f32[2,1536]{1,0:T(2,128)}, u32[]{:S(2)}) copy-start(f32[2,1536]{1,0:T(2,128)} %get-tuple-element.291) | copy-start | bytes 36868 | tf_op jit(solution)/shard_map/while
  343.8 89.2 %copy-start.2 = (f32[2,2048]{1,0:T(2,128)S(1)}, f32[2,2048]{1,0:T(2,128)}, u32[]{:S(2)}) copy-start(f32[2,2048]{1,0:T(2,128)} %get-tuple-element.292) | copy-start | bytes 49156 | tf_op jit(solution)/shard_map/while
  498.0 60.9 %copy-start.6 = (f32[512]{0:T(512)S(1)}, f32[512]{0:T(512)}, u32[]{:S(2)}) copy-start(f32[512]{0:T(512)} %get-tuple-element.287) | copy-start | bytes 6148 | tf_op jit(solution)/shard_map/while
  498.1 60.9 %copy-start.7 = (f32[512]{0:T(512)S(1)}, f32[512]{0:T(512)}, u32[]{:S(2)}) copy-start(f32[512]{0:T(512)} %get-tuple-element.288) | copy-start | bytes 6148 | tf_op jit(solution)/shard_map/while
  498.1 62.2 %copy-start.3 = (f32[2,1536]{1,0:T(2,128)S(1)}, f32[2,1536]{1,0:T(2,128)}, u32[]{:S(2)}) copy-start(f32[2,1536]{1,0:T(2,128)} %get-tuple-element.290) | copy-start | bytes 36868 | tf_op jit(solution)/shard_map/while
  498.1 62.2 %copy-start.4 = (f32[2,1536]{1,0:T(2,128)S(1)}, f32[2,1536]{1,0:T(2,128)}, u32[]{:S(2)}) copy-start(f32[2,1536]{1,0:T(2,128)} %get-tuple-element.291) | copy-start | bytes 36868 | tf_op jit(solution)/shard_map/while
  507.4 89.2 %copy-start.2 = (f32[2,2048]{1,0:T(2,128)S(1)}, f32[2,2048]{1,0:T(2,128)}, u32[]{:S(2)}) copy-start(f32[2,2048]{1,0:T(2,128)} %get-tuple-element.292) | copy-start | bytes 49156 | tf_op jit(solution)/shard_map/while
  661.7 0.6 copy-start
  661.7 0.6 copy-start.1
  661.7 0.6 copy-start.5
where the time goes:
time: 665 us; the launch traced here: 663 us
  blocking collectives  554 us (83%)
  matrix products  82.1 us (12%)
  loops' own time  14.4 us (2%)
  other arithmetic  7.76 us (1%)
    psum x4, blocking collectives, iterate(): lax.psum((primal_move, dual_move), ('scen', 'row', 'col'))  250 us
    psum x4, blocking collectives, iterate(): first_grad = lax.psum(first_part, ('scen', 'row'))  149 us
    psum x4, blocking collectives, iterate(): activity = lax.psum(activity_part, 'col')  95.3 us
    psum x4, blocking collectives, iterate(): recourse_grad = lax.psum(recourse_part, 'row')  59.8 us
    dot_general x8, matrix products, forward(): jnp.einsum('src,skc->skr', matrix, stacked, preferred_element_type=jnp.fl...  45.4 us
    dot_general x8, matrix products, backward(): jnp.einsum('src,skr->skc', matrix, stacked, preferred_element_type=jnp.fl...  36.7 us
    another operation x1, loops' own time, local(): lax.fori_loop(0, ITERS, iterate, start)  14.4 us

commit v1 on v0

v1 whole, which is shorter than its diff:
```python
import jax
import jax.numpy as jnp
from jax import lax
from jax.experimental import pallas as pl
from jax.experimental.pallas import tpu as pltpu
from jax.sharding import PartitionSpec as P

MESH = pl.DeviceIdType.MESH
ITERS = 4
STEP_SCALE = 0.8
EPSILON = 1e-06
SCEN, ROWS, FIRST, REC = 2, 2048, 512, 1536
COLS = FIRST + REC
WIDE = 512
TRAIL = 128


def split_rows(value):
    upper = value.astype(jnp.bfloat16).astype(jnp.float32)
    return jnp.concatenate([upper, value - upper], 0).astype(jnp.bfloat16)


def kernel(
    tech_hbm,
    rec_hbm,
    first_cost_hbm,
    rec_cost_hbm,
    demand_hbm,
    first_upper_hbm,
    rec_upper_hbm,
    first_start_hbm,
    rec_start_hbm,
    dual_start_hbm,
    first_out,
    rec_out,
    dual_out,
    weight_out,
    mat,
    mat_t,
    first_cost,
    rec_cost,
    demand,
    first_upper,
    rec_upper,
    first_now,
    rec_now,
    duals,
    sums,
    weight,
    tech_slot,
    rec_slot,
    act_slot,
    move_slot,
    load_sem,
    small_sem,
    tech_send,
    tech_recv,
    rec_send,
    rec_recv,
    act_send,
    act_recv,
    move_send,
    move_recv,
):
    scen, row, col = lax.axis_index("scen"), lax.axis_index("row"), lax.axis_index("col")
    place = scen * 4 + row

    row_peers = [{"row": lax.rem(row + d, 4)} for d in (2, 1, 3)]
    col_peers = [{"col": lax.rem(col + d, 8)} for d in (4, 5, 3, 2, 6, 1, 7)]
    block_peers = [
        {"scen": lax.rem(scen + d, 4), "row": lax.rem(row + e, 4)}
        for d in (2, 1, 3, 0)
        for e in (2, 1, 3, 0)
        if d or e
    ]

    barrier = pltpu.get_barrier_semaphore()
    for peer in block_peers + col_peers:
        pl.semaphore_signal(barrier, inc=1, device_id=peer, device_id_type=MESH)

    pieces = []
    for part in range(4):
        for s in range(SCEN):
            if part == 0:
                source = tech_hbm.at[s]
            else:
                source = rec_hbm.at[s, :, pl.ds((part - 1) * WIDE, WIDE)]
            pieces.append(
                pltpu.make_async_copy(
                    source, mat.at[s, :, pl.ds(part * WIDE, WIDE)], load_sem.at[part, s]
                )
            )
    smalls = [
        pltpu.make_async_copy(dual_start_hbm, duals, small_sem.at[0]),
        pltpu.make_async_copy(demand_hbm, demand, small_sem.at[1]),
        pltpu.make_async_copy(rec_cost_hbm, rec_cost, small_sem.at[2]),
        pltpu.make_async_copy(rec_upper_hbm, rec_upper, small_sem.at[3]),
        pltpu.make_async_copy(rec_start_hbm, rec_now, small_sem.at[4]),
        pltpu.make_async_copy(first_cost_hbm, first_cost, small_sem.at[5]),
        pltpu.make_async_copy(first_upper_hbm, first_upper, small_sem.at[6]),
        pltpu.make_async_copy(first_start_hbm, first_now, small_sem.at[7]),
    ]
    for copy in smalls[:1] + pieces + smalls[1:]:
        copy.start()

    def send(slot, mine, peers, send_sem, recv_sem):
        for peer in peers:
            pltpu.make_async_remote_copy(
                src_ref=slot.at[mine],
                dst_ref=slot.at[mine],
                send_sem=send_sem,
                recv_sem=recv_sem,
                device_id=peer,
                device_id_type=MESH,
            ).start()

    def wait_bytes(slot, count, sem):
        view = slot.at[pl.ds(0, count)]
        pltpu.make_async_copy(view, view, sem).wait()

    def back(left, s, part):
        out = jnp.dot(
            left,
            mat[s, :, pl.ds(part * WIDE, WIDE)],
            preferred_element_type=jnp.float32,
        )
        return out[s : s + 1] + out[2 + s : 3 + s]

    def back_part(left, it, part):
        if part == 0:
            total = back(left, 0, 0) + back(left, 1, 0)
            tech_slot[it, pl.ds(place, 1)] = total.reshape(1, 1, WIDE)
            send(
                tech_slot.at[it], place, block_peers, tech_send.at[it], tech_recv.at[it]
            )
        else:
            for s in range(SCEN):
                rec_slot[it, part - 1, row, pl.ds(s, 1)] = back(left, s, part)
            send(
                rec_slot.at[it, part - 1],
                row,
                row_peers,
                rec_send.at[it, part - 1],
                rec_recv.at[it, part - 1],
            )

    def turn(s, part):
        for k in range(2):
            cols = pl.ds(part * WIDE + k * 256, 256)
            mat_t[s, cols, :] = mat[s, :, cols].T

    smalls[0].wait()
    weight[...] = jnp.ones_like(weight)
    left = split_rows(duals[...])
    for part in range(4):
        pieces[part * 2].wait()
        pieces[part * 2 + 1].wait()
        if part == 0:
            pl.semaphore_wait(barrier, 22)
        back_part(left, 0, part)
        if part < 3:
            turn(0, part)
            turn(1, part)
    turn(0, 3)
    turn(1, 3)
    for copy in smalls[1:]:
        copy.wait()

    def forward(left, part):
        for s in range(SCEN):
            out = jnp.dot(
                left,
                mat_t[s, pl.ds(part * WIDE, WIDE), :],
                preferred_element_type=jnp.float32,
            )
            sums[s] = out if part == 1 else sums[s] + out

    def iterate(it, carry):
        now = weight[:, 0:1]
        step_primal = STEP_SCALE / now
        step_dual = STEP_SCALE * now
        rec_move = jnp.zeros((1, 1), jnp.float32)
        first_move = jnp.zeros((1, 1), jnp.float32)
        for part in (1, 2, 0, 3):
            if part == 0:
                wait_bytes(tech_slot.at[it], 15, tech_recv.at[it])
                grad = tech_slot[it, 0]
                for p in range(1, 16):
                    grad = grad + tech_slot[it, p]
                old = first_now[...]
                new = jnp.clip(
                    old - step_primal * (first_cost[...] - grad), 0.0, first_upper[...]
                )
                first_now[...] = new
                bar = jnp.broadcast_to(2.0 * new - old, (SCEN, FIRST))
                first_move = jnp.sum((new - old) ** 2, keepdims=True)
            else:
                wait_bytes(rec_slot.at[it, part - 1], 3, rec_recv.at[it, part - 1])
                grad = rec_slot[it, part - 1, 0]
                for p in range(1, 4):
                    grad = grad + rec_slot[it, part - 1, p]
                cols = pl.ds((part - 1) * WIDE, WIDE)
                old = rec_now[:, cols]
                new = jnp.clip(
                    old - step_primal * (rec_cost[:, cols] - grad), 0.0, rec_upper[:, cols]
                )
                rec_now[:, cols] = new
                bar = 2.0 * new - old
                rec_move = rec_move + jnp.sum((new - old) ** 2, keepdims=True)
            forward(split_rows(bar), part)
        for s in range(SCEN):
            act_slot[it, col, pl.ds(s, 1), pl.ds(0, ROWS)] = sums[s, s : s + 1] + sums[s, 2 + s : 3 + s]
        act_slot[it, col, :, pl.ds(ROWS, TRAIL)] = jnp.broadcast_to(
            0.25 * rec_move + 0.0625 * first_move, (SCEN, TRAIL)
        )
        send(act_slot.at[it], col, col_peers, act_send.at[it], act_recv.at[it])
        wait_bytes(act_slot.at[it], 7, act_recv.at[it])
        activity = act_slot[it, 0]
        for p in range(1, 8):
            activity = activity + act_slot[it, p]
        old = duals[...]
        new = jnp.maximum(0.0, old + step_dual * (demand[...] - activity[:, :ROWS]))
        duals[...] = new
        dual_move = jnp.sum((new - old) ** 2, keepdims=True)
        move_slot[it, pl.ds(place, 1)] = jnp.concatenate(
            [jnp.broadcast_to(dual_move, (1, TRAIL)), activity[0:1, ROWS:]], 0
        ).reshape(1, 2, TRAIL)
        send(move_slot.at[it], place, block_peers, move_send.at[it], move_recv.at[it])

        @pl.when(it < ITERS - 1)
        def _():
            left = split_rows(duals[...])
            for part in range(4):
                back_part(left, it + 1, part)

        wait_bytes(move_slot.at[it], 15, move_recv.at[it])
        moves = move_slot[it, 0]
        for p in range(1, 16):
            moves = moves + move_slot[it, p]
        before = weight[...]
        weight[...] = jnp.exp(
            0.25 * jnp.log((moves[0:1] + EPSILON) / (moves[1:2] + EPSILON))
            + 0.5 * jnp.log(before)
        )
        return carry

    lax.fori_loop(0, ITERS, iterate, 0)

    first_out[...] = first_now[...]
    rec_out[...] = rec_now[...]
    dual_out[...] = duals[...]
    weight_out[...] = weight[...]

    def drain(it, carry):
        wait_bytes(tech_slot.at[it], 15, tech_send.at[it])
        for part in range(3):
            wait_bytes(rec_slot.at[it, part], 3, rec_send.at[it, part])
        wait_bytes(act_slot.at[it], 7, act_send.at[it])
        wait_bytes(move_slot.at[it], 15, move_send.at[it])
        return carry

    lax.fori_loop(0, ITERS, drain, 0)


def local(
    tech_matrix,
    recourse_matrix,
    first_cost,
    recourse_cost,
    demand,
    first_upper,
    recourse_upper,
    first_start,
    recourse_start,
    dual_start,
):
    f32 = jnp.float32
    dma = pltpu.SemaphoreType.DMA
    first, rec, duals, weight = pl.pallas_call(
        kernel,
        out_shape=(
            jax.ShapeDtypeStruct((1, FIRST), f32),
            jax.ShapeDtypeStruct((SCEN, REC), f32),
            jax.ShapeDtypeStruct((SCEN, ROWS), f32),
            jax.ShapeDtypeStruct((1, TRAIL), f32),
        ),
        in_specs=[pl.BlockSpec(memory_space=pltpu.HBM)] * 10,
        out_specs=[pl.BlockSpec(memory_space=pltpu.VMEM)] * 4,
        scratch_shapes=[
            pltpu.VMEM((SCEN, ROWS, COLS), jnp.bfloat16),
            pltpu.VMEM((SCEN, COLS, ROWS), jnp.bfloat16),
            pltpu.VMEM((1, FIRST), f32),
            pltpu.VMEM((SCEN, REC), f32),
            pltpu.VMEM((SCEN, ROWS), f32),
            pltpu.VMEM((1, FIRST), f32),
            pltpu.VMEM((SCEN, REC), f32),
            pltpu.VMEM((1, FIRST), f32),
            pltpu.VMEM((SCEN, REC), f32),
            pltpu.VMEM((SCEN, ROWS), f32),
            pltpu.VMEM((SCEN, 2 * SCEN, ROWS), f32),
            pltpu.VMEM((1, TRAIL), f32),
            pltpu.VMEM((ITERS, 16, 1, FIRST), f32),
            pltpu.VMEM((ITERS, 3, 4, SCEN, WIDE), f32),
            pltpu.VMEM((ITERS, 8, SCEN, ROWS + TRAIL), f32),
            pltpu.VMEM((ITERS, 16, 2, TRAIL), f32),
            dma((4, SCEN)),
            dma((8,)),
            dma((ITERS,)),
            dma((ITERS,)),
            dma((ITERS, 3)),
            dma((ITERS, 3)),
            dma((ITERS,)),
            dma((ITERS,)),
            dma((ITERS,)),
            dma((ITERS,)),
        ],
        compiler_params=pltpu.CompilerParams(
            collective_id=0, has_side_effects=True, vmem_limit_bytes=48 * 2**20
        ),
    )(
        tech_matrix,
        recourse_matrix,
        first_cost.reshape(1, FIRST),
        recourse_cost,
        demand,
        first_upper.reshape(1, FIRST),
        recourse_upper,
        first_start.reshape(1, FIRST),
        recourse_start,
        dual_start,
    )
    return first.reshape(FIRST), rec, duals, weight[0, 0]


def solution(mesh):
    in_specs = (
        P("scen", "row", "col"),
        P("scen", "row", "col"),
        P("col"),
        P("scen", "col"),
        P("scen", "row"),
        P("col"),
        P("scen", "col"),
        P("col"),
        P("scen", "col"),
        P("scen", "row"),
    )
    out_specs = (P("col"), P("scen", "col"), P("scen", "row"), P())
    return jax.shard_map(local, mesh=mesh, in_specs=in_specs, out_specs=out_specs, check_vma=False)
```

time: 665 us -> 73.8 us (0.11)
  blocking collectives: 554 us -> 0 us
  matrix products: 82.1 us -> 0 us
  Pallas kernels: 0 us -> 61.8 us
  loops' own time: 14.4 us -> 0 us
  other arithmetic: 7.76 us -> 0 us
    psum x16 -> x0, blocking collectives: 554 us -> none  [the longest x4 250 us: iterate(): lax.psum((primal_move, dual_move), ('scen', 'row', 'col'))]
    dot_general x16 -> x0, matrix products: 82.1 us -> none  [the longest x8 45.4 us: forward(): jnp.einsum('src,skc->skr', matrix, stacked, preferred_element_type=jnp.fl...]
    pallas_call x0 -> x1, Pallas kernels: none -> 61.8 us  [local(): pl.pallas_call(kernel, out_shape=(jax.ShapeDtypeStruct((1, FIRST), f32),...]
    another operation x1 -> x0, loops' own time: 14.4 us -> none  [local(): lax.fori_loop(0, ITERS, iterate, start)]
    reduce_sum x12 -> x0, other arithmetic: 7.46 us -> none  [the longest x4 2.54 us: iterate(): dual_full = jnp.sum((duals_new - duals_now) ** 2)]
    unnamed x9 -> x21, local copies, waits for them, and re-layouts: 2.7 us -> 9.56 us
where the time goes in v1:
time: 73.8 us; the launch traced here: 73.2 us
  Pallas kernels  61.8 us (84%)
  local copies, waits for them, and re-layouts  9.56 us (13%)
  between operations  1.83 us (2%)
    pallas_call x1, Pallas kernels, local(): pl.pallas_call(kernel, out_shape=(jax.ShapeDtypeStruct((1, FIRST), f32),...  61.8 us
    unnamed x21, local copies, waits for them, and re-layouts  9.56 us

profile of v1, /device:TPU:0, one launch (start us, length us, event | category | flops | bytes accessed | tf_op | source)
XLA Modules:
  0.0 73.2 jit_solution(14595428403921973604)
XLA Ops:
  0.6 0.0 copy-start
  0.6 2.2 %copy-done = bf16[2,2048,512]{2,1,0:T(8,128)(2,1)S(1)} copy-done((bf16[2,2048,512]{2,1,0:T(8,128)(2,1)S(1)}, bf16[2,2048,512]{2,1,0:T(8,128)(2,1)}, u32[]{:S(2)}) %copy-start) | copy-done | bytes 4194328
  2.8 0.0 copy-start.1
  2.8 0.7 copy-done.1
  3.5 0.0 copy-start.2
  3.5 0.7 copy-done.2
  4.3 0.0 copy-start.3
  4.3 0.7 copy-done.3
  5.0 0.0 copy-start.4
  5.0 0.7 copy-done.4
  5.7 0.0 copy-start.5
  5.7 0.7 copy-done.5
  6.4 0.0 copy-start.6
  6.4 0.7 copy-done.6
  7.1 0.0 copy-start.7
  7.1 0.7 copy-done.7
  7.7 0.0 copy-start.8
  7.7 0.7 copy-done.8
  8.4 61.8 %shard_map.129 = (f32[1,512]{1,0:T(1,128)S(1)}, f32[2,1536]{1,0:T(2,128)S(1)}, f32[2,2048]{1,0:T(2,128)S(1)}, f32[1,128]{1,0:T(1,128)S(1)}) custom-call(bf16[2,2048,512]{2,1,0:T(8,128)(2,1)S(1)} %copy-done, bf16[2,2048,1536]{2,1,0:T(8,128)(2,1)} %rec_hbm.1, f32[1,512]{1,0:T(1,128)S(1)} %bitcast.6, f32[2,1536]{1,0:T(2,128)S(1)} %copy-done.3, ...), custom_call_target="tpu_custom_call" | custom-call | tf_op jit(solution)/shard_map/pallas_call | solution.py:279
  70.3 0.6 copy.18
  70.9 0.6 copy.19
  71.5 0.6 copy.20
Async XLA Ops:
  0.6 2.2 %copy-start = (bf16[2,2048,512]{2,1,0:T(8,128)(2,1)S(1)}, bf16[2,2048,512]{2,1,0:T(8,128)(2,1)}, u32[]{:S(2)}) copy-start(bf16[2,2048,512]{2,1,0:T(8,128)(2,1)} %tech_hbm.1) | copy-start | bytes 12582916
  2.8 0.7 copy-start.1
  3.5 0.7 copy-start.2
  4.3 0.7 copy-start.3
  5.0 0.7 copy-start.4
  5.7 0.7 copy-start.5
  6.4 0.7 copy-start.6
  7.1 0.7 copy-start.7
  7.7 0.7 copy-start.8

commit v2 on v1

--- a/solution.py
+++ b/solution.py
@@ -13,6 +13,7 @@
 COLS = FIRST + REC
 WIDE = 512
 TRAIL = 128
+EARLY = ((0, 0), (0, 1), (1, 0), (1, 1), (2, 0))
 
 
 def split_rows(value):
@@ -47,6 +48,7 @@
     duals,
     sums,
     weight,
+    tech_part,
     tech_slot,
     rec_slot,
     act_slot,
@@ -124,25 +126,20 @@
             mat[s, :, pl.ds(part * WIDE, WIDE)],
             preferred_element_type=jnp.float32,
         )
-        return out[s : s + 1] + out[2 + s : 3 + s]
-
-    def back_part(left, it, part):
-        if part == 0:
-            total = back(left, 0, 0) + back(left, 1, 0)
-            tech_slot[it, pl.ds(place, 1)] = total.reshape(1, 1, WIDE)
-            send(
-                tech_slot.at[it], place, block_peers, tech_send.at[it], tech_recv.at[it]
-            )
-        else:
-            for s in range(SCEN):
-                rec_slot[it, part - 1, row, pl.ds(s, 1)] = back(left, s, part)
-            send(
-                rec_slot.at[it, part - 1],
-                row,
-                row_peers,
-                rec_send.at[it, part - 1],
-                rec_recv.at[it, part - 1],
-            )
+        return out[0:1] + out[1:2]
+
+    def send_tech(it, total):
+        tech_slot[it, pl.ds(place, 1)] = total.reshape(1, 1, WIDE)
+        send(tech_slot.at[it], place, block_peers, tech_send.at[it], tech_recv.at[it])
+
+    def send_rec(it, part):
+        send(
+            rec_slot.at[it, part - 1],
+            row,
+            row_peers,
+            rec_send.at[it, part - 1],
+            rec_recv.at[it, part - 1],
+        )
 
     def turn(s, part):
         for k in range(2):
@@ -151,36 +148,42 @@
 
     smalls[0].wait()
     weight[...] = jnp.ones_like(weight)
-    left = split_rows(duals[...])
+    left = [split_rows(duals[s : s + 1, :]) for s in range(SCEN)]
+    total = None
     for part in range(4):
-        pieces[part * 2].wait()
-        pieces[part * 2 + 1].wait()
+        for s in range(SCEN):
+            pieces[part * 2 + s].wait()
+            out = back(left[s], s, part)
+            if part == 0:
+                total = out if s == 0 else total + out
+            else:
+                rec_slot[0, part - 1, row, pl.ds(s, 1)] = out
+            if (part, s) in EARLY:
+                turn(s, part)
         if part == 0:
             pl.semaphore_wait(barrier, 22)
-        back_part(left, 0, part)
-        if part < 3:
-            turn(0, part)
-            turn(1, part)
-    turn(0, 3)
-    turn(1, 3)
+            send_tech(0, total)
+        else:
+            send_rec(0, part)
+    for part in (1, 2, 0, 3):
+        for s in range(SCEN):
+            if (part, s) not in EARLY:
+                turn(s, part)
     for copy in smalls[1:]:
         copy.wait()
 
-    def forward(left, part):
-        for s in range(SCEN):
-            out = jnp.dot(
-                left,
-                mat_t[s, pl.ds(part * WIDE, WIDE), :],
-                preferred_element_type=jnp.float32,
-            )
-            sums[s] = out if part == 1 else sums[s] + out
+    def forward(left, s, part):
+        return jnp.dot(
+            left,
+            mat_t[s, pl.ds(part * WIDE, WIDE), :],
+            preferred_element_type=jnp.float32,
+        )
 
     def iterate(it, carry):
         now = weight[:, 0:1]
         step_primal = STEP_SCALE / now
         step_dual = STEP_SCALE * now
-        rec_move = jnp.zeros((1, 1), jnp.float32)
-        first_move = jnp.zeros((1, 1), jnp.float32)
+        move = jnp.zeros((1, WIDE), jnp.float32)
         for part in (1, 2, 0, 3):
             if part == 0:
                 wait_bytes(tech_slot.at[it], 15, tech_recv.at[it])
@@ -193,7 +196,7 @@
                 )
                 first_now[...] = new
                 bar = jnp.broadcast_to(2.0 * new - old, (SCEN, FIRST))
-                first_move = jnp.sum((new - old) ** 2, keepdims=True)
+                move = move + 0.0625 * (new - old) ** 2
             else:
                 wait_bytes(rec_slot.at[it, part - 1], 3, rec_recv.at[it, part - 1])
                 grad = rec_slot[it, part - 1, 0]
@@ -206,42 +209,69 @@
                 )
                 rec_now[:, cols] = new
                 bar = 2.0 * new - old
-                rec_move = rec_move + jnp.sum((new - old) ** 2, keepdims=True)
-            forward(split_rows(bar), part)
-        for s in range(SCEN):
-            act_slot[it, col, pl.ds(s, 1), pl.ds(0, ROWS)] = sums[s, s : s + 1] + sums[s, 2 + s : 3 + s]
-        act_slot[it, col, :, pl.ds(ROWS, TRAIL)] = jnp.broadcast_to(
-            0.25 * rec_move + 0.0625 * first_move, (SCEN, TRAIL)
+                square = 0.25 * (new - old) ** 2
+                move = move + square[0:1] + square[1:2]
+            left = split_rows(bar)
+            if part == 3:
+                spread = move[:, 0:TRAIL]
+                for k in range(1, WIDE // TRAIL):
+                    spread = spread + move[:, k * TRAIL : (k + 1) * TRAIL]
+                for s in range(SCEN):
+                    act_slot[it, s, col, :, pl.ds(ROWS, TRAIL)] = spread
+            for s in range(SCEN):
+                out = forward(left, s, part)
+                if part == 1:
+                    sums[s] = out
+                elif part != 3:
+                    sums[s] = sums[s] + out
+                else:
+                    out = sums[s] + out
+                    act_slot[it, s, col, :, pl.ds(0, ROWS)] = out[s : s + 1] + out[2 + s : 3 + s]
+                    send(
+                        act_slot.at[it, s], col, col_peers, act_send.at[it, s], act_recv.at[it, s]
+                    )
+
+        def dual_step(s):
+            wait_bytes(act_slot.at[it, s], 7, act_recv.at[it, s])
+            activity = act_slot[it, s, 0]
+            for p in range(1, 8):
+                activity = activity + act_slot[it, s, p]
+            old = duals[s : s + 1, :]
+            new = jnp.maximum(
+                0.0, old + step_dual * (demand[s : s + 1, :] - activity[:, :ROWS])
+            )
+            duals[s : s + 1, :] = new
+            square = (new - old) ** 2
+            spread = square[:, 0:TRAIL]
+            for k in range(1, ROWS // TRAIL):
+                spread = spread + square[:, k * TRAIL : (k + 1) * TRAIL]
+            return new, spread, activity[:, ROWS:]
+
+        new_0, spread_0, _ = dual_step(0)
+        left_0 = split_rows(new_0)
+        tech_part[...] = back(left_0, 0, 0)
+        new_1, spread_1, primal = dual_step(1)
+        move_slot[it, pl.ds(place, 1)] = jnp.concatenate([spread_0 + spread_1, primal], 0).reshape(
+            1, 2, TRAIL
         )
-        send(act_slot.at[it], col, col_peers, act_send.at[it], act_recv.at[it])
-        wait_bytes(act_slot.at[it], 7, act_recv.at[it])
-        activity = act_slot[it, 0]
-        for p in range(1, 8):
-            activity = activity + act_slot[it, p]
-        old = duals[...]
-        new = jnp.maximum(0.0, old + step_dual * (demand[...] - activity[:, :ROWS]))
-        duals[...] = new
-        dual_move = jnp.sum((new - old) ** 2, keepdims=True)
-        move_slot[it, pl.ds(place, 1)] = jnp.concatenate(
-            [jnp.broadcast_to(dual_move, (1, TRAIL)), activity[0:1, ROWS:]], 0
-        ).reshape(1, 2, TRAIL)
         send(move_slot.at[it], place, block_peers, move_send.at[it], move_recv.at[it])
 
         @pl.when(it < ITERS - 1)
         def _():
-            left = split_rows(duals[...])
-            for part in range(4):
-                back_part(left, it + 1, part)
+            left = [split_rows(duals[s : s + 1, :]) for s in range(SCEN)]
+            send_tech(it + 1, tech_part[...] + back(left[1], 1, 0))
+            for part in (1, 2, 3):
+                for s in range(SCEN):
+                    rec_slot[it + 1, part - 1, row, pl.ds(s, 1)] = back(left[s], s, part)
+                send_rec(it + 1, part)
 
         wait_bytes(move_slot.at[it], 15, move_recv.at[it])
         moves = move_slot[it, 0]
         for p in range(1, 16):
             moves = moves + move_slot[it, p]
+        moves = jnp.sum(moves, 1, keepdims=True) + EPSILON
         before = weight[...]
-        weight[...] = jnp.exp(
-            0.25 * jnp.log((moves[0:1] + EPSILON) / (moves[1:2] + EPSILON))
-            + 0.5 * jnp.log(before)
-        )
+        weight[...] = jnp.exp(0.25 * jnp.log(moves[0:1] / moves[1:2]) + 0.5 * jnp.log(before))
         return carry
 
     lax.fori_loop(0, ITERS, iterate, 0)
@@ -249,17 +279,31 @@
     first_out[...] = first_now[...]
     rec_out[...] = rec_now[...]
     dual_out[...] = duals[...]
-    weight_out[...] = weight[...]
+    weight_out[...] = weight[:, 0:1]
 
     def drain(it, carry):
         wait_bytes(tech_slot.at[it], 15, tech_send.at[it])
         for part in range(3):
             wait_bytes(rec_slot.at[it, part], 3, rec_send.at[it, part])
-        wait_bytes(act_slot.at[it], 7, act_send.at[it])
+        for s in range(SCEN):
+            wait_bytes(act_slot.at[it, s], 7, act_send.at[it, s])
         wait_bytes(move_slot.at[it], 15, move_send.at[it])
         return carry
 
     lax.fori_loop(0, ITERS, drain, 0)
+
+
+def place_outputs(first, rec, duals, weight, first_out, rec_out, dual_out, weight_out, sem):
+    copies = [
+        pltpu.make_async_copy(first, first_out, sem.at[0]),
+        pltpu.make_async_copy(rec, rec_out, sem.at[1]),
+        pltpu.make_async_copy(duals, dual_out, sem.at[2]),
+        pltpu.make_async_copy(weight, weight_out, sem.at[3]),
+    ]
+    for copy in copies:
+        copy.start()
+    for copy in copies:
+        copy.wait()
 
 
 def local(
@@ -282,7 +326,7 @@
             jax.ShapeDtypeStruct((1, FIRST), f32),
             jax.ShapeDtypeStruct((SCEN, REC), f32),
             jax.ShapeDtypeStruct((SCEN, ROWS), f32),
-            jax.ShapeDtypeStruct((1, TRAIL), f32),
+            jax.ShapeDtypeStruct((1, 1), f32),
         ),
         in_specs=[pl.BlockSpec(memory_space=pltpu.HBM)] * 10,
         out_specs=[pl.BlockSpec(memory_space=pltpu.VMEM)] * 4,
@@ -299,9 +343,10 @@
             pltpu.VMEM((SCEN, ROWS), f32),
             pltpu.VMEM((SCEN, 2 * SCEN, ROWS), f32),
             pltpu.VMEM((1, TRAIL), f32),
+            pltpu.VMEM((1, FIRST), f32),
             pltpu.VMEM((ITERS, 16, 1, FIRST), f32),
             pltpu.VMEM((ITERS, 3, 4, SCEN, WIDE), f32),
-            pltpu.VMEM((ITERS, 8, SCEN, ROWS + TRAIL), f32),
+            pltpu.VMEM((ITERS, SCEN, 8, 1, ROWS + TRAIL), f32),
             pltpu.VMEM((ITERS, 16, 2, TRAIL), f32),
             dma((4, SCEN)),
             dma((8,)),
@@ -309,13 +354,13 @@
             dma((ITERS,)),
             dma((ITERS, 3)),
             dma((ITERS, 3)),
-            dma((ITERS,)),
-            dma((ITERS,)),
+            dma((ITERS, SCEN)),
+            dma((ITERS, SCEN)),
             dma((ITERS,)),
             dma((ITERS,)),
         ],
         compiler_params=pltpu.CompilerParams(
-            collective_id=0, has_side_effects=True, vmem_limit_bytes=48 * 2**20
+            collective_id=0, has_side_effects=True, vmem_limit_bytes=63 * 2**20
         ),
     )(
         tech_matrix,
@@ -329,7 +374,20 @@
         recourse_start,
         dual_start,
     )
-    return first.reshape(FIRST), rec, duals, weight[0, 0]
+    outs = pl.pallas_call(
+        place_outputs,
+        out_shape=(
+            jax.ShapeDtypeStruct((1, FIRST), f32),
+            jax.ShapeDtypeStruct((SCEN, REC), f32),
+            jax.ShapeDtypeStruct((SCEN, ROWS), f32),
+            jax.ShapeDtypeStruct((1, 1), f32),
+        ),
+        in_specs=[pl.BlockSpec(memory_space=pl.ANY)] * 4,
+        out_specs=[pl.BlockSpec(memory_space=pltpu.HBM)] * 4,
+        scratch_shapes=[dma((4,))],
+        compiler_params=pltpu.CompilerParams(vmem_limit_bytes=63 * 2**20),
+    )(first, rec, duals, weight)
+    return outs[0].reshape(FIRST), outs[1], outs[2], outs[3].reshape(())
 
 
 def solution(mesh):

time: 73.8 us -> 62.4 us (0.85)
  local copies, waits for them, and re-layouts: 9.56 us -> 0 us
  between operations: 1.83 us -> 0.64 us
    unnamed x21 -> x0, local copies, waits for them, and re-layouts: 9.56 us -> none
    pallas_call x1, Pallas kernels: 61.8 us -> 58.9 us  [local(): pl.pallas_call(kernel, out_shape=(jax.ShapeDtypeStruct((1, FIRST), f32),...]
    pallas_call x0 -> x1, Pallas kernels: none -> 2.69 us  [local(): pl.pallas_call(place_outputs, out_shape=(jax.ShapeDtypeStruct((1, FIRST),...]
where the time goes in v2:
time: 62.4 us; the launch traced here: 62.2 us
  Pallas kernels  61.6 us (99%)
  between operations  0.64 us (1%)
    pallas_call x1, Pallas kernels, local(): pl.pallas_call(kernel, out_shape=(jax.ShapeDtypeStruct((1, FIRST), f32),...  58.9 us
    pallas_call x1, Pallas kernels, local(): pl.pallas_call(place_outputs, out_shape=(jax.ShapeDtypeStruct((1, FIRST),...  2.69 us

profile of v2, /device:TPU:0, one launch (start us, length us, event | category | flops | bytes accessed | tf_op | source)
XLA Modules:
  0.0 62.2 jit_solution(1446452309860988343)
XLA Ops:
  0.6 58.9 %shard_map.129 = (f32[1,512]{1,0:T(1,128)}, f32[2,1536]{1,0:T(2,128)}, f32[2,2048]{1,0:T(2,128)}, f32[1,1]{1,0:T(1,128)}) custom-call(bf16[2,2048,512]{2,1,0:T(8,128)(2,1)} %tech_hbm.1, bf16[2,2048,1536]{2,1,0:T(8,128)(2,1)} %rec_hbm.1, f32[1,512]{1,0:T(1,128)} %bitcast.5, f32[2,1536]{1,0:T(2,128)} %rec_cost_hbm.1, f32[2,2048]{1,0:T(2,128)} %demand_hbm.1, ...), custom_call_target="tpu_custom_call" | custom-call | tf_op jit(solution)/shard_map/pallas_call | solution.py:323
  59.5 2.7 %shard_map.130 = (f32[1,512]{1,0:T(1,128)}, f32[2,1536]{1,0:T(2,128)}, f32[2,2048]{1,0:T(2,128)}, f32[1,1]{1,0:T(1,128)}) custom-call(f32[1,512]{1,0:T(1,128)} %get-tuple-element.12.first, f32[2,1536]{1,0:T(2,128)} %get-tuple-element.13.rec, f32[2,2048]{1,0:T(2,128)} %get-tuple-element.14.duals, f32[1,1]{1,0:T(1,128)} %get-tuple-element.15.weight), custom_call_target="tpu_custom_call" | custom-call | tf_op jit(solution)/shard_map/pallas_call | solution.py:377

commit v3 on v2

--- a/solution.py
+++ b/solution.py
@@ -12,6 +12,7 @@
 SCEN, ROWS, FIRST, REC = 2, 2048, 512, 1536
 COLS = FIRST + REC
 WIDE = 512
+PLACE = (2, 0, 1, 3)
 TRAIL = 128
 EARLY = ((0, 0), (0, 1), (1, 0), (1, 1), (2, 0))
 
@@ -32,9 +33,9 @@
     first_start_hbm,
     rec_start_hbm,
     dual_start_hbm,
-    first_out,
-    rec_out,
-    dual_out,
+    first_now,
+    rec_now,
+    duals,
     weight_out,
     mat,
     mat_t,
@@ -43,9 +44,6 @@
     demand,
     first_upper,
     rec_upper,
-    first_now,
-    rec_now,
-    duals,
     sums,
     weight,
     tech_part,
@@ -89,7 +87,7 @@
                 source = rec_hbm.at[s, :, pl.ds((part - 1) * WIDE, WIDE)]
             pieces.append(
                 pltpu.make_async_copy(
-                    source, mat.at[s, :, pl.ds(part * WIDE, WIDE)], load_sem.at[part, s]
+                    source, mat.at[s, :, pl.ds(PLACE[part] * WIDE, WIDE)], load_sem.at[part, s]
                 )
             )
     smalls = [
@@ -123,7 +121,7 @@
     def back(left, s, part):
         out = jnp.dot(
             left,
-            mat[s, :, pl.ds(part * WIDE, WIDE)],
+            mat[s, :, pl.ds(PLACE[part] * WIDE, WIDE)],
             preferred_element_type=jnp.float32,
         )
         return out[0:1] + out[1:2]
@@ -143,11 +141,11 @@
 
     def turn(s, part):
         for k in range(2):
-            cols = pl.ds(part * WIDE + k * 256, 256)
+            cols = pl.ds(PLACE[part] * WIDE + k * 256, 256)
             mat_t[s, cols, :] = mat[s, :, cols].T
 
     smalls[0].wait()
-    weight[...] = jnp.ones_like(weight)
+    weight[...] = jnp.zeros_like(weight)
     left = [split_rows(duals[s : s + 1, :]) for s in range(SCEN)]
     total = None
     for part in range(4):
@@ -172,64 +170,64 @@
     for copy in smalls[1:]:
         copy.wait()
 
-    def forward(left, s, part):
+    def forward(bar, s, first, count):
         return jnp.dot(
-            left,
-            mat_t[s, pl.ds(part * WIDE, WIDE), :],
+            split_rows(bar),
+            mat_t[s, pl.ds(first * WIDE, count * WIDE), :],
             preferred_element_type=jnp.float32,
         )
 
+    def wide(value, count):
+        return jnp.concatenate([value] * (count // TRAIL), 1)
+
     def iterate(it, carry):
-        now = weight[:, 0:1]
-        step_primal = STEP_SCALE / now
-        step_dual = STEP_SCALE * now
-        move = jnp.zeros((1, WIDE), jnp.float32)
-        for part in (1, 2, 0, 3):
-            if part == 0:
-                wait_bytes(tech_slot.at[it], 15, tech_recv.at[it])
-                grad = tech_slot[it, 0]
-                for p in range(1, 16):
-                    grad = grad + tech_slot[it, p]
-                old = first_now[...]
-                new = jnp.clip(
-                    old - step_primal * (first_cost[...] - grad), 0.0, first_upper[...]
-                )
-                first_now[...] = new
-                bar = jnp.broadcast_to(2.0 * new - old, (SCEN, FIRST))
-                move = move + 0.0625 * (new - old) ** 2
-            else:
-                wait_bytes(rec_slot.at[it, part - 1], 3, rec_recv.at[it, part - 1])
-                grad = rec_slot[it, part - 1, 0]
-                for p in range(1, 4):
-                    grad = grad + rec_slot[it, part - 1, p]
-                cols = pl.ds((part - 1) * WIDE, WIDE)
-                old = rec_now[:, cols]
-                new = jnp.clip(
-                    old - step_primal * (rec_cost[:, cols] - grad), 0.0, rec_upper[:, cols]
-                )
-                rec_now[:, cols] = new
-                bar = 2.0 * new - old
-                square = 0.25 * (new - old) ** 2
-                move = move + square[0:1] + square[1:2]
-            left = split_rows(bar)
-            if part == 3:
-                spread = move[:, 0:TRAIL]
-                for k in range(1, WIDE // TRAIL):
-                    spread = spread + move[:, k * TRAIL : (k + 1) * TRAIL]
-                for s in range(SCEN):
-                    act_slot[it, s, col, :, pl.ds(ROWS, TRAIL)] = spread
-            for s in range(SCEN):
-                out = forward(left, s, part)
-                if part == 1:
-                    sums[s] = out
-                elif part != 3:
-                    sums[s] = sums[s] + out
-                else:
-                    out = sums[s] + out
-                    act_slot[it, s, col, :, pl.ds(0, ROWS)] = out[s : s + 1] + out[2 + s : 3 + s]
-                    send(
-                        act_slot.at[it, s], col, col_peers, act_send.at[it, s], act_recv.at[it, s]
-                    )
+        log_weight = weight[...]
+        step_primal = wide(STEP_SCALE * jnp.exp(-log_weight), WIDE)
+        step_dual = wide(STEP_SCALE * jnp.exp(log_weight), ROWS)
+
+        def rec_step(part):
+            wait_bytes(rec_slot.at[it, part - 1], 3, rec_recv.at[it, part - 1])
+            grad = rec_slot[it, part - 1, 0]
+            for p in range(1, 4):
+                grad = grad + rec_slot[it, part - 1, p]
+            cols = pl.ds((part - 1) * WIDE, WIDE)
+            old = rec_now[:, cols]
+            new = jnp.clip(
+                old - step_primal * (rec_cost[:, cols] - grad), 0.0, rec_upper[:, cols]
+            )
+            rec_now[:, cols] = new
+            square = 0.25 * (new - old) ** 2
+            return 2.0 * new - old, square[0:1] + square[1:2]
+
+        def first_step():
+            wait_bytes(tech_slot.at[it], 15, tech_recv.at[it])
+            grad = tech_slot[it, 0]
+            for p in range(1, 16):
+                grad = grad + tech_slot[it, p]
+            old = first_now[...]
+            new = jnp.clip(old - step_primal * (first_cost[...] - grad), 0.0, first_upper[...])
+            first_now[...] = new
+            return jnp.broadcast_to(2.0 * new - old, (SCEN, FIRST)), 0.0625 * (new - old) ** 2
+
+        bar, move = rec_step(1)
+        for s in range(SCEN):
+            sums[s] = forward(bar, s, 0, 1)
+        bar_2, move_2 = rec_step(2)
+        bar_0, move_0 = first_step()
+        bar = jnp.concatenate([bar_2, bar_0], 1)
+        move = move + move_2 + move_0
+        for s in range(SCEN):
+            sums[s] = sums[s] + forward(bar, s, 1, 2)
+        bar, move_3 = rec_step(3)
+        move = move + move_3
+        spread = move[:, 0:TRAIL]
+        for k in range(1, WIDE // TRAIL):
+            spread = spread + move[:, k * TRAIL : (k + 1) * TRAIL]
+        for s in range(SCEN):
+            act_slot[it, s, col, :, pl.ds(ROWS, TRAIL)] = spread
+            out = sums[s] + forward(bar, s, 3, 1)
+            act_slot[it, s, col, :, pl.ds(0, ROWS)] = out[s : s + 1] + out[2 + s : 3 + s]
+            send(act_slot.at[it, s], col, col_peers, act_send.at[it, s], act_recv.at[it, s])
 
         def dual_step(s):
             wait_bytes(act_slot.at[it, s], 7, act_recv.at[it, s])
@@ -269,17 +267,13 @@
         moves = move_slot[it, 0]
         for p in range(1, 16):
             moves = moves + move_slot[it, p]
-        moves = jnp.sum(moves, 1, keepdims=True) + EPSILON
-        before = weight[...]
-        weight[...] = jnp.exp(0.25 * jnp.log(moves[0:1] / moves[1:2]) + 0.5 * jnp.log(before))
+        logs = jnp.log(jnp.broadcast_to(jnp.sum(moves, 1, keepdims=True), (2, TRAIL)) + EPSILON)
+        weight[...] = 0.25 * (logs[0:1] - logs[1:2]) + 0.5 * log_weight
         return carry
 
     lax.fori_loop(0, ITERS, iterate, 0)
 
-    first_out[...] = first_now[...]
-    rec_out[...] = rec_now[...]
-    dual_out[...] = duals[...]
-    weight_out[...] = weight[:, 0:1]
+    weight_out[...] = jnp.exp(weight[:, 0:1])
 
     def drain(it, carry):
         wait_bytes(tech_slot.at[it], 15, tech_send.at[it])
@@ -338,9 +332,6 @@
             pltpu.VMEM((SCEN, ROWS), f32),
             pltpu.VMEM((1, FIRST), f32),
             pltpu.VMEM((SCEN, REC), f32),
-            pltpu.VMEM((1, FIRST), f32),
-            pltpu.VMEM((SCEN, REC), f32),
-            pltpu.VMEM((SCEN, ROWS), f32),
             pltpu.VMEM((SCEN, 2 * SCEN, ROWS), f32),
             pltpu.VMEM((1, TRAIL), f32),
             pltpu.VMEM((1, FIRST), f32),
@@ -360,19 +351,24 @@
             dma((ITERS,)),
         ],
         compiler_params=pltpu.CompilerParams(
-            collective_id=0, has_side_effects=True, vmem_limit_bytes=63 * 2**20
+            collective_id=0, has_side_effects=True, vmem_limit_bytes=44 * 2**20
         ),
     )(
-        tech_matrix,
-        recourse_matrix,
-        first_cost.reshape(1, FIRST),
-        recourse_cost,
-        demand,
-        first_upper.reshape(1, FIRST),
-        recourse_upper,
-        first_start.reshape(1, FIRST),
-        recourse_start,
-        dual_start,
+        *(
+            pltpu.with_memory_space_constraint(array, pltpu.HBM)
+            for array in (
+                tech_matrix,
+                recourse_matrix,
+                first_cost.reshape(1, FIRST),
+                recourse_cost,
+                demand,
+                first_upper.reshape(1, FIRST),
+                recourse_upper,
+                first_start.reshape(1, FIRST),
+                recourse_start,
+                dual_start,
+            )
+        )
     )
     outs = pl.pallas_call(
         place_outputs,
@@ -385,7 +381,7 @@
         in_specs=[pl.BlockSpec(memory_space=pl.ANY)] * 4,
         out_specs=[pl.BlockSpec(memory_space=pltpu.HBM)] * 4,
         scratch_shapes=[dma((4,))],
-        compiler_params=pltpu.CompilerParams(vmem_limit_bytes=63 * 2**20),
+        compiler_params=pltpu.CompilerParams(vmem_limit_bytes=1 * 2**20),
     )(first, rec, duals, weight)
     return outs[0].reshape(FIRST), outs[1], outs[2], outs[3].reshape(())
 

time: 62.4 us -> 59.8 us (0.958)
  Pallas kernels: 61.6 us -> 59 us
    pallas_call x1, Pallas kernels: 2.69 us -> 1.28 us  [local(): pl.pallas_call(place_outputs, out_shape=(jax.ShapeDtypeStruct((1, FIRST),...]
    pallas_call x1, Pallas kernels: 58.9 us -> 57.7 us  [local(): pl.pallas_call(kernel, out_shape=(jax.ShapeDtypeStruct((1, FIRST), f32),...]
where the time goes in v3:
time: 59.8 us; the launch traced here: 59.6 us
  Pallas kernels  59 us (99%)
  between operations  0.64 us (1%)
    pallas_call x1, Pallas kernels, local(): pl.pallas_call(kernel, out_shape=(jax.ShapeDtypeStruct((1, FIRST), f32),...  57.7 us
    pallas_call x1, Pallas kernels, local(): pl.pallas_call(place_outputs, out_shape=(jax.ShapeDtypeStruct((1, FIRST),...  1.28 us

profile of v3, /device:TPU:0, one launch (start us, length us, event | category | flops | bytes accessed | tf_op | source)
XLA Modules:
  0.0 59.6 jit_solution(14761490379460979221)
XLA Ops:
  0.6 57.7 %shard_map.129 = (f32[1,512]{1,0:T(1,128)S(1)}, f32[2,1536]{1,0:T(2,128)S(1)}, f32[2,2048]{1,0:T(2,128)S(1)}, f32[1,1]{1,0:T(1,128)}) custom-call(bf16[2,2048,512]{2,1,0:T(8,128)(2,1)} %tech_hbm.1, bf16[2,2048,1536]{2,1,0:T(8,128)(2,1)} %rec_hbm.1, f32[1,512]{1,0:T(1,128)} %bitcast.5, f32[2,1536]{1,0:T(2,128)} %rec_cost_hbm.1, f32[2,2048]{1,0:T(2,128)} %demand_hbm.1, ...), custom_call_target="tpu_custom_call" | custom-call | tf_op jit(solution)/shard_map/pallas_call | solution.py:317
  58.4 1.3 %shard_map.130 = (f32[1,512]{1,0:T(1,128)}, f32[2,1536]{1,0:T(2,128)}, f32[2,2048]{1,0:T(2,128)}, f32[1,1]{1,0:T(1,128)}) custom-call(f32[1,512]{1,0:T(1,128)S(1)} %get-tuple-element.12.first, f32[2,1536]{1,0:T(2,128)S(1)} %get-tuple-element.13.rec, f32[2,2048]{1,0:T(2,128)S(1)} %get-tuple-element.14.duals, f32[1,1]{1,0:T(1,128)} %get-tuple-element.15.weight), custom_call_target="tpu_custom_call" | custom-call | tf_op jit(solution)/shard_map/pallas_call | solution.py:373

commit v4 on v3

--- a/solution.py
+++ b/solution.py
@@ -46,6 +46,7 @@
     rec_upper,
     sums,
     weight,
+    slope,
     tech_part,
     tech_slot,
     rec_slot,
@@ -180,21 +181,25 @@
     def wide(value, count):
         return jnp.concatenate([value] * (count // TRAIL), 1)
 
+    def rec_slope(it, part):
+        wait_bytes(rec_slot.at[it, part - 1], 3, rec_recv.at[it, part - 1])
+        grad = rec_slot[it, part - 1, 0]
+        for p in range(1, 4):
+            grad = grad + rec_slot[it, part - 1, p]
+        return rec_cost[:, pl.ds((part - 1) * WIDE, WIDE)] - grad
+
+    slope[...] = rec_slope(0, 1)
+
     def iterate(it, carry):
         log_weight = weight[...]
         step_primal = wide(STEP_SCALE * jnp.exp(-log_weight), WIDE)
         step_dual = wide(STEP_SCALE * jnp.exp(log_weight), ROWS)
 
         def rec_step(part):
-            wait_bytes(rec_slot.at[it, part - 1], 3, rec_recv.at[it, part - 1])
-            grad = rec_slot[it, part - 1, 0]
-            for p in range(1, 4):
-                grad = grad + rec_slot[it, part - 1, p]
             cols = pl.ds((part - 1) * WIDE, WIDE)
             old = rec_now[:, cols]
-            new = jnp.clip(
-                old - step_primal * (rec_cost[:, cols] - grad), 0.0, rec_upper[:, cols]
-            )
+            fall = slope[...] if part == 1 else rec_slope(it, part)
+            new = jnp.clip(old - step_primal * fall, 0.0, rec_upper[:, cols])
             rec_now[:, cols] = new
             square = 0.25 * (new - old) ** 2
             return 2.0 * new - old, square[0:1] + square[1:2]
@@ -262,6 +267,7 @@
                 for s in range(SCEN):
                     rec_slot[it + 1, part - 1, row, pl.ds(s, 1)] = back(left[s], s, part)
                 send_rec(it + 1, part)
+            slope[...] = rec_slope(it + 1, 1)
 
         wait_bytes(move_slot.at[it], 15, move_recv.at[it])
         moves = move_slot[it, 0]
@@ -334,6 +340,7 @@
             pltpu.VMEM((SCEN, REC), f32),
             pltpu.VMEM((SCEN, 2 * SCEN, ROWS), f32),
             pltpu.VMEM((1, TRAIL), f32),
+            pltpu.VMEM((SCEN, WIDE), f32),
             pltpu.VMEM((1, FIRST), f32),
             pltpu.VMEM((ITERS, 16, 1, FIRST), f32),
             pltpu.VMEM((ITERS, 3, 4, SCEN, WIDE), f32),

time: 59.8 us -> 60.1 us (level)
  no operation moved by 1% of the time
where the time goes in v4:
time: 60.1 us; the launch traced here: 59.9 us
  Pallas kernels  59.2 us (99%)
  between operations  0.64 us (1%)
    pallas_call x1, Pallas kernels, local(): pl.pallas_call(kernel, out_shape=(jax.ShapeDtypeStruct((1, FIRST), f32),...  58 us
    pallas_call x1, Pallas kernels, local(): pl.pallas_call(place_outputs, out_shape=(jax.ShapeDtypeStruct((1, FIRST),...  1.28 us

profile of v4, /device:TPU:0, one launch (start us, length us, event | category | flops | bytes accessed | tf_op | source)
XLA Modules:
  0.0 59.9 jit_solution(12438184103291647995)
XLA Ops:
  0.6 58.0 %shard_map.129 = (f32[1,512]{1,0:T(1,128)S(1)}, f32[2,1536]{1,0:T(2,128)S(1)}, f32[2,2048]{1,0:T(2,128)S(1)}, f32[1,1]{1,0:T(1,128)}) custom-call(bf16[2,2048,512]{2,1,0:T(8,128)(2,1)} %tech_hbm.1, bf16[2,2048,1536]{2,1,0:T(8,128)(2,1)} %rec_hbm.1, f32[1,512]{1,0:T(1,128)} %bitcast.5, f32[2,1536]{1,0:T(2,128)} %rec_cost_hbm.1, f32[2,2048]{1,0:T(2,128)} %demand_hbm.1, ...), custom_call_target="tpu_custom_call" | custom-call | tf_op jit(solution)/shard_map/pallas_call | solution.py:323
  58.6 1.3 %shard_map.130 = (f32[1,512]{1,0:T(1,128)}, f32[2,1536]{1,0:T(2,128)}, f32[2,2048]{1,0:T(2,128)}, f32[1,1]{1,0:T(1,128)}) custom-call(f32[1,512]{1,0:T(1,128)S(1)} %get-tuple-element.12.first, f32[2,1536]{1,0:T(2,128)S(1)} %get-tuple-element.13.rec, f32[2,2048]{1,0:T(2,128)S(1)} %get-tuple-element.14.duals, f32[1,1]{1,0:T(1,128)} %get-tuple-element.15.weight), custom_call_target="tpu_custom_call" | custom-call | tf_op jit(solution)/shard_map/pallas_call | solution.py:380

commit v5 on v3

--- a/solution.py
+++ b/solution.py
@@ -14,6 +14,7 @@
 WIDE = 512
 PLACE = (2, 0, 1, 3)
 TRAIL = 128
+AHEAD = 3
 EARLY = ((0, 0), (0, 1), (1, 0), (1, 1), (2, 0))
 
 
@@ -100,7 +101,7 @@
         pltpu.make_async_copy(first_upper_hbm, first_upper, small_sem.at[6]),
         pltpu.make_async_copy(first_start_hbm, first_now, small_sem.at[7]),
     ]
-    for copy in smalls[:1] + pieces + smalls[1:]:
+    for copy in smalls[:1] + pieces[:AHEAD] + smalls[1:]:
         copy.start()
 
     def send(slot, mine, peers, send_sem, recv_sem):
@@ -151,6 +152,8 @@
     for part in range(4):
         for s in range(SCEN):
             pieces[part * 2 + s].wait()
+            if part * 2 + s + AHEAD < len(pieces):
+                pieces[part * 2 + s + AHEAD].start()
             out = back(left[s], s, part)
             if part == 0:
                 total = out if s == 0 else total + out

time: 59.8 us -> 60 us (level)
  no operation moved by 1% of the time
where the time goes in v5:
time: 60 us; the launch traced here: 59.8 us
  Pallas kernels  59.2 us (99%)
  between operations  0.64 us (1%)
    pallas_call x1, Pallas kernels, local(): pl.pallas_call(kernel, out_shape=(jax.ShapeDtypeStruct((1, FIRST), f32),...  57.9 us
    pallas_call x1, Pallas kernels, local(): pl.pallas_call(place_outputs, out_shape=(jax.ShapeDtypeStruct((1, FIRST),...  1.28 us

profile of v5, /device:TPU:0, one launch (start us, length us, event | category | flops | bytes accessed | tf_op | source)
XLA Modules:
  0.0 59.8 jit_solution(13546616369463540698)
XLA Ops:
  0.6 57.9 %shard_map.129 = (f32[1,512]{1,0:T(1,128)S(1)}, f32[2,1536]{1,0:T(2,128)S(1)}, f32[2,2048]{1,0:T(2,128)S(1)}, f32[1,1]{1,0:T(1,128)}) custom-call(bf16[2,2048,512]{2,1,0:T(8,128)(2,1)} %tech_hbm.1, bf16[2,2048,1536]{2,1,0:T(8,128)(2,1)} %rec_hbm.1, f32[1,512]{1,0:T(1,128)} %bitcast.5, f32[2,1536]{1,0:T(2,128)} %rec_cost_hbm.1, f32[2,2048]{1,0:T(2,128)} %demand_hbm.1, ...), custom_call_target="tpu_custom_call" | custom-call | tf_op jit(solution)/shard_map/pallas_call | solution.py:320
  58.5 1.3 %shard_map.130 = (f32[1,512]{1,0:T(1,128)}, f32[2,1536]{1,0:T(2,128)}, f32[2,2048]{1,0:T(2,128)}, f32[1,1]{1,0:T(1,128)}) custom-call(f32[1,512]{1,0:T(1,128)S(1)} %get-tuple-element.12.first, f32[2,1536]{1,0:T(2,128)S(1)} %get-tuple-element.13.rec, f32[2,2048]{1,0:T(2,128)S(1)} %get-tuple-element.14.duals, f32[1,1]{1,0:T(1,128)} %get-tuple-element.15.weight), custom_call_target="tpu_custom_call" | custom-call | tf_op jit(solution)/shard_map/pallas_call | solution.py:376
